TPU v7x, 32 devices: a whole 2x2x4 slice. The times are simulated.
32 devices in a mesh: dp: 4 (over y, core), space: 8 (over z, x).
Axes of the slice: x: 2, y: 2, z: 4, core: 2. Of those that a mesh axis runs over, the one named last changes fastest.
Arguments:
- snapshot: bfloat16 [4, 32, 64, 1024], P('dp', 'space'), may hold values from -6 to 6
- conv_one: bfloat16 [864, 128], replicated, may hold values from -0.21875 to 0.21875
- conv_two: bfloat16 [3456, 256], replicated, may hold values from -0.0546875 to 0.0546875
- cotangent: bfloat16 [4, 256, 8, 128], P('dp', 'space'), may hold values from -0.046875 to 0.046875
Outputs:
- latent: bfloat16 [4, 256, 8, 128], P('dp', 'space')
- grad_one: float32 [128, 864], P('space')
- grad_two: float32 [256, 3456], P('space')
All inputs are finite; a program needn't handle non-finite values.
Results may differ from a plain program's by a relative error of at most 0.0049.
Values may be sent and summed in bfloat16 or wider, within the bound.
No kernel may reach another device: no remote copies, remote signals or barrier semaphores. Data moves between devices by JAX's collectives and lax.ppermute only.
A program may use at most 64 MiB of HBM per device.

v0:
```python
import jax
import jax.numpy as jnp
from jax import lax
from jax.sharding import PartitionSpec as P


def from_behind(block, axis, distance):
    devices = range(lax.axis_size(axis))
    route = [(i - distance, i) for i in devices if i - distance in devices]
    return lax.ppermute(block, axis, route)


def patches(padded, out_x, out_y, out_z):
    channels = padded.shape[3]
    grown = jnp.pad(padded, ((0, 1), (0, 1), (0, 1), (0, 0)))
    phased = grown.reshape(out_x + 1, 2, out_y + 1, 2, out_z + 1, 2, channels)
    pieces = []
    for tap_x in range(3):
        for tap_y in range(3):
            for tap_z in range(3):
                start = (tap_x // 2, tap_x % 2, tap_y // 2, tap_y % 2, tap_z // 2, tap_z % 2, 0)
                limit = (
                    tap_x // 2 + out_x,
                    tap_x % 2 + 1,
                    tap_y // 2 + out_y,
                    tap_y % 2 + 1,
                    tap_z // 2 + out_z,
                    tap_z % 2 + 1,
                    channels,
                )
                pieces.append(
                    lax.slice(phased, start, limit).reshape(out_x, out_y, out_z, channels)
                )
    stacked = jnp.concatenate(pieces, axis=3)
    return stacked.reshape(out_x * out_y * out_z, 27 * channels)


def fold_axis(blocks, space, tap):
    first_tap = lax.index_in_dim(blocks, 0, tap, keepdims=False)
    middle_tap = lax.index_in_dim(blocks, 1, tap, keepdims=False)
    last_tap = lax.index_in_dim(blocks, 2, tap, keepdims=False)
    after = [(0, 0)] * first_tap.ndim
    before = [(0, 0)] * first_tap.ndim
    after[space] = (0, 1)
    before[space] = (1, 0)
    even_cells = jnp.pad(first_tap, after) + jnp.pad(last_tap, before)
    odd_cells = jnp.pad(middle_tap, after)
    joined = jnp.stack([even_cells, odd_cells], axis=space + 1)
    shape = list(even_cells.shape)
    shape[space] = 2 * shape[space]
    return joined.reshape(shape)


def spread_taps(back_rows, out_x, out_y, out_z):
    channels = back_rows.shape[1] // 27
    blocks = back_rows.reshape(out_x, out_y, out_z, 3, 3, 3, channels)
    blocks = fold_axis(blocks, 2, 5)
    blocks = fold_axis(blocks, 1, 4)
    blocks = fold_axis(blocks, 0, 3)
    return blocks[: 2 * out_x + 1, : 2 * out_y + 1, : 2 * out_z + 1]


def silu_slope(values):
    logistic = jax.nn.sigmoid(values)
    return logistic * (1.0 + values * (1.0 - logistic))


def on_device(snapshot, conv_one, conv_two, cotangent):
    in_width = conv_one.shape[0] // 27
    mid_width = conv_one.shape[1]
    out_width = conv_two.shape[1]
    slab_cells = snapshot[0]
    extent_x, extent_y = (slab_cells.shape[0], slab_cells.shape[1])
    fine_grid = slab_cells.reshape(extent_x, extent_y, -1, in_width)
    extent_z = fine_grid.shape[2]
    half_x, half_y, half_z = (extent_x // 2, extent_y // 2, extent_z // 2)
    quarter_x, quarter_y, quarter_z = (extent_x // 4, extent_y // 4, extent_z // 4)
    lower_plane = from_behind(slab_cells[extent_x - 1 :], "space", 1)
    joined = jnp.concatenate(
        [lower_plane.reshape(1, extent_y, extent_z, in_width), fine_grid], axis=0
    )
    padded = jnp.pad(joined, ((0, 0), (1, 0), (1, 0), (0, 0)))
    patch_one = patches(padded, half_x, half_y, half_z)
    hidden_pre = jnp.dot(patch_one, conv_one, preferred_element_type=jnp.float32)
    hidden = jax.nn.silu(hidden_pre).astype(jnp.bfloat16)
    act_grid = hidden.reshape(half_x, half_y, half_z, mid_width)
    act_lower = from_behind(act_grid[half_x - 1 :], "space", 1)
    act_pad = jnp.pad(
        jnp.concatenate([act_lower, act_grid], axis=0), ((0, 0), (1, 0), (1, 0), (0, 0))
    )
    patch_two = patches(act_pad, quarter_x, quarter_y, quarter_z)
    latent_rows = jnp.dot(patch_two, conv_two, preferred_element_type=jnp.float32).astype(
        jnp.bfloat16
    )
    latent_slab = latent_rows.reshape(quarter_x, -1, out_width).transpose(2, 0, 1)
    latent = lax.all_to_all(latent_slab, "space", split_axis=0, concat_axis=1, tiled=True)[None]
    upstream = lax.all_to_all(cotangent[0], "space", split_axis=1, concat_axis=0, tiled=True)
    grad_grid = upstream.transpose(1, 2, 0)
    grad_rows = grad_grid.reshape(-1, out_width)
    term_two = lax.dot_general(
        patch_two, grad_rows, (((0,), (0,)), ((), ())), preferred_element_type=jnp.float32
    ).T
    back_rows = lax.dot_general(
        grad_rows, conv_two, (((1,), (1,)), ((), ())), preferred_element_type=jnp.float32
    )
    grad_pad = spread_taps(back_rows, quarter_x, quarter_y, quarter_z)
    upper_plane = from_behind(grad_pad[0:1, 1:, 1:], "space", -1)
    grad_act = jnp.concatenate(
        [grad_pad[1:half_x, 1:, 1:], grad_pad[half_x:, 1:, 1:] + upper_plane], axis=0
    )
    grad_pre = (grad_act.reshape(-1, mid_width) * silu_slope(hidden_pre)).astype(jnp.bfloat16)
    term_one = lax.dot_general(
        patch_one, grad_pre, (((0,), (0,)), ((), ())), preferred_element_type=jnp.float32
    ).T
    summed = lax.psum((term_one, term_two), "dp")
    shares = (
        lax.psum_scatter(summed[0], "space", scatter_dimension=0, tiled=True),
        lax.psum_scatter(summed[1], "space", scatter_dimension=0, tiled=True),
    )
    return (latent, shares[0], shares[1])


def solution(mesh):
    placed = (P("dp", "space", None, None), P(), P(), P("dp", "space", None, None))
    return jax.shard_map(
        on_device,
        mesh=mesh,
        in_specs=placed,
        out_specs=(P("dp", "space", None, None), P("space", None), P("space", None)),
        check_vma=False,
    )
```

profile of v0, /device:TPU:0, one launch (start us, length us, event | category | flops | bytes accessed | tf_op | source)
XLA Modules:
  0.0 328.7 jit_solution(645473647259848543)
XLA Ops:
  7.2 1.6 copy.254
  8.8 7.3 %all-to-all-start.1 = ((bf16[32,8,128]{2,0,1:T(8,128)(2,1)}), bf16[32,8,128]{2,0,1:T(8,128)(2,1)S(1)}, u32[]{:S(2)}, u32[]{:S(2)}) async-start(bf16[32,8,128]{2,0,1:T(8,128)(2,1)} %bitcast.179), calls=%async_computation.1 | async-start | bytes 131072 | tf_op jit(solution)/shard_map/all_to_all | solution.py:97
  16.1 1.5 copy.144
  18.3 3.9 %collective-permute-start = (bf16[1,64,1024]{1,2,0:T(8,128)(2,1)}, bf16[1,64,1024]{1,2,0:T(8,128)(2,1)S(1)}, u32[]{:S(2)}, u32[]{:S(2)}) collective-permute-start(bf16[1,64,1024]{1,2,0:T(8,128)(2,1)} %slice_bitcast_fusion.9), channel_id=1, source_target_pairs={{0,1},{1,2},{2,3},{3,4},{4,5},{5,6},{6,7},{8,9},{9,10},{10,11},{11... | collective-permute-start | bytes 393224 | tf_op jit(solution)/shard_map/ppermute | solution.py:10
  29.6 1.2 fusion.11
  30.8 1.5 collective-permute-start.2
  32.3 1.3 pad_maximum_fusion.2
  33.6 3.9 %copy.225 = bf16[5,64,32,32]{3,1,2,0:T(8,128)(2,1)} copy(bf16[5,64,32,32]{1,3,2,0:T(8,128)(2,1)} %pad_maximum_fusion.2) | data formatting | bytes 1310720
  37.6 4.9 %pad.74 = bf16[6,66,34,32]{3,1,2,0:T(8,128)(2,1)} pad(bf16[5,64,32,32]{3,1,2,0:T(8,128)(2,1)} %copy.225, bf16[]{:T(256)} %constant.6.clone.1), padding=0_1x1_1x1_1x0_0 | pad | bytes 1517058 | tf_op jit(solution)/shard_map/jit(_pad)/pad | solution.py:15
  42.4 8.2 %reshape.213 = bf16[3,2,33,2,17,2,32]{6,3,2,5,4,1,0:T(2,128)(2,1)} reshape(bf16[6,66,34,32]{3,1,2,0:T(8,128)(2,1)} %pad.74) | data formatting | bytes 1723392 | tf_op jit(solution)/shard_map/reshape | solution.py:16
  50.6 15.0 %fusion.9 = (bf16[2,1,32,1,16,1,32]{6,3,2,5,4,1,0:T(2,128)(2,1)S(1)}, bf16[2,1,32,1,16,1,32]{6,3,2,5,4,1,0:T(2,128)(2,1)S(1)}, bf16[2,1,32,1,16,1,32]{6,3,2,5,4,...) fusion(bf16[3,2,33,2,17,2,32]{6,3,2,5,4,1,0:T(2,128)(2,1)} %res, ...), kind=kLoop, calls=%fused_computation.67 | loop fusion | bytes 2490368 | tf_op jit(solution)/shard_map/slice | solution.py:32
  65.6 5.1 %fusion.10 = (bf16[2,1,32,1,16,1,32]{6,3,2,5,4,1,0:T(2,128)(2,1)S(1)}, bf16[2,1,32,1,16,1,32]{6,3,2,5,4,1,0:T(2,128)(2,1)S(1)}, bf16[2,1,32,1,16,1,32]{6,3,2,5,4...) fusion(bf16[3,2,33,2,17,2,32]{6,3,2,5,4,1,0:T(2,128)(2,1)S(1)} , ...), kind=kLoop, calls=%fused_computation.68 | loop fusion | bytes 1048576 | tf_op jit(solution)/shard_map/slice | solution.py:32
  78.8 1.0 copy.167
  84.9 1.0 copy.173
  85.9 1.0 copy.154
  90.0 1.0 copy.150
  91.0 1.0 copy.151
  94.1 7.9 %concatenate.153 = bf16[1024,864]{1,0:T(8,128)(2,1)} concatenate(bf16[1024,32]{1,0:T(8,128)(2,1)} %bitcast.208, bf16[1024,32]{1,0:T(8,128)(2,1)} %bitcast.209, bf16[1024,32]{1,0:T(8,128)(2,1)} %bitcast.210, bf16[1024,32]{1,0:T(8,128)(2,1)} %bitcast.211, bf16[1024,32]{1,0:T(8,128)(2,1)} %bitcast.212, bf16[1024,32]{1,0:T(8,128)(2,1)} %bitcast.213, bf16[1024,32]{1,0:T(8,128)(2,1)} %bitcast.214, ...), dimensions={1} | concatenate | bytes 3538944 | tf_op jit(solution)/shard_map/concatenate | solution.py:34
  102.1 1.9 slice_add_fusion
  103.9 1.4 pad_maximum_fusion.4
  106.4 4.8 %collective-permute-start.1 = (bf16[1,32,16,128]{3,0,2,1:T(2,128)(2,1)S(1)}, bf16[1,32,16,128]{3,0,2,1:T(2,128)(2,1)S(1)}, u32[]{:S(2)}, u32[]{:S(2)}) collective-permute-start(bf16[1,32,16,128]{3,0,2,1:T(2,128)(2,1)S(1)} %copy.174), channel_id=1, source_target_pairs={{0,1},{1,2},{2,3},{3,4},{4,5},{5,6},{6,7},{8,9},{9,10},{10,11},{11... | collective-permute-start | bytes 393224 | tf_op jit(solution)/shard_map/ppermute | solution.py:10
  111.5 3.3 %collective-permute-done.1 = bf16[1,32,16,128]{3,0,2,1:T(2,128)(2,1)S(1)} collective-permute-done((bf16[1,32,16,128]{3,0,2,1:T(2,128)(2,1)S(1)}, bf16[1,32,16,128]{3,0,2,1:T(2,128)(2,1)S(1)}, u32[]{:S(2)}, u32[]{:S(2)}) %collective-permute-start.1) | collective-permute-done | bytes 131104 | tf_op jit(solution)/shard_map/ppermute | solution.py:10
  117.5 2.5 convolution_bitcast_fusion
  119.9 5.2 %copy.190 = f32[256,3456]{1,0:T(8,128)} copy(f32[256,3456]{0,1:T(8,128)} %convolution_bitcast_fusion) | data formatting | bytes 7077888
  125.2 2.7 fusion.14
  128.0 78.8 %reduce-scatter.7.cloned.1.call-done = f32[32,3456]{1,0:T(8,128)} async-done(((f32[256,3456]{1,0:T(8,128)}), f32[32,3456]{1,0:T(8,128)}) %reduce-scatter.7.cloned.1.call-update) | async-done | bytes 442384
  206.8 2.8 copy.191
  211.4 11.2 %all_to_all.33 = bf16[8,2,2048]{2,1,0:T(2,128)(2,1)S(1)} all-to-all(bf16[8,2,2048]{2,1,0:T(2,128)(2,1)S(1)} %reshape.227), channel_id=1, replica_groups=mesh['dp'=4,'space'=8] {'space'}, dimensions={0} | all-to-all | bytes 131072 | tf_op jit(solution)/shard_map/all_to_all | solution.py:96
  223.4 48.2 %reduce-scatter.5.cloned.1.call-done = f32[16,864]{1,0:T(8,128)} async-done(((f32[128,864]{1,0:T(8,128)}), f32[16,864]{1,0:T(8,128)}) %reduce-scatter.5.cloned.1.call-update) | async-done | bytes 55312 | tf_op jit(solution)/shard_map/reduce_scatter | solution.py:117
  271.6 12.4 %psum.16 = f32[16,864]{1,0:T(8,128)} all-reduce(f32[16,864]{1,0:T(8,128)} %reduce-scatter.5.cloned.1.call-done), channel_id=1, replica_groups=mesh['dp'=4,'space'=8] {'dp'}, use_global_device_ids=true, to_apply=%region_0.1 | all-reduce | flops 13824 | bytes 110592 | tf_op jit(solution)/shard_map/psum | solution.py:115
  284.0 35.4 %all-reduce.15.cloned.1.call-done = f32[32,3456]{0,1:T(8,128)} async-done(((f32[32,3456]{0,1:T(8,128)}), f32[32,3456]{0,1:T(8,128)}) %all-reduce.15.cloned.1.call-update) | async-done | bytes 442384 | tf_op jit(solution)/shard_map/psum | solution.py:115
  319.4 2.7 copy.188
  (102 shorter events, 32.5 us)
Async XLA Ops:
  7.2 15.9 %copy-start = (bf16[3456,256]{1,0:T(8,128)(2,1)S(1)}, bf16[3456,256]{1,0:T(8,128)(2,1)}, u32[]{:S(2)}) copy-start(bf16[3456,256]{1,0:T(8,128)(2,1)} %param.6) | copy-start | bytes 5308420
  8.8 14.2 %all-to-all-start.1 = ((bf16[32,8,128]{2,0,1:T(8,128)(2,1)}), bf16[32,8,128]{2,0,1:T(8,128)(2,1)S(1)}, u32[]{:S(2)}, u32[]{:S(2)}) async-start(bf16[32,8,128]{2,0,1:T(8,128)(2,1)} %bitcast.179), calls=%async_computation.1 | async-start | bytes 131072 | tf_op jit(solution)/shard_map/all_to_all | solution.py:97
  16.0 190.8 %reduce-scatter.7.cloned.1.call-start = ((), (), s32[]{:S(2)}) async-start(), calls=%async_computation.6 | async-start | bytes 3981312
  18.3 14.0 %collective-permute-start = (bf16[1,64,1024]{1,2,0:T(8,128)(2,1)}, bf16[1,64,1024]{1,2,0:T(8,128)(2,1)S(1)}, u32[]{:S(2)}, u32[]{:S(2)}) collective-permute-start(bf16[1,64,1024]{1,2,0:T(8,128)(2,1)} %slice_bitcast_fusion.9), channel_id=1, source_target_pairs={{0,1},{1,2},{2,3},{3,4},{4,5},{5,6},{6,7},{8,9},{9,10},{10,11},{11... | collective-permute-start | bytes 393224 | tf_op jit(solution)/shard_map/ppermute | solution.py:10
  28.6 1.0 copy-start.3
  30.8 71.2 %collective-permute-start.2 = (f32[1,32,16,128]{3,0,2,1:T(1,128)}, f32[1,32,16,128]{3,0,2,1:T(1,128)}, u32[]{:S(2)}, u32[]{:S(2)}) collective-permute-start(f32[1,32,16,128]{3,0,2,1:T(1,128)} %get-tuple-element.52), channel_id=1, source_target_pairs={{1,0},{2,1},{3,2},{4,3},{5,4},{6,5},{7,6},{9,8},{10,9},{11,10},{12... | collective-permute-start | bytes 786440 | tf_op jit(solution)/shard_map/ppermute | solution.py:10
  50.6 15.0 %copy-start.1 = (bf16[3,2,33,2,17,2,32]{6,3,2,5,4,1,0:T(2,128)(2,1)S(1)}, bf16[3,2,33,2,17,2,32]{6,3,2,5,4,1,0:T(2,128)(2,1)}, u32[]{:S(2)}) copy-start(bf16[3,2,33,2,17,2,32]{6,3,2,5,4,1,0:T(2,128)(2,1)} %reshape.213) | copy-start | bytes 2585092
  102.0 3.4 %copy-start.2 = (bf16[1024,864]{1,0:T(8,128)(2,1)S(1)}, bf16[1024,864]{1,0:T(8,128)(2,1)}, u32[]{:S(2)}) copy-start(bf16[1024,864]{1,0:T(8,128)(2,1)} %concatenate.153) | copy-start | bytes 5308420
  102.0 3.4 %copy-start.4 = (bf16[864,128]{1,0:T(8,128)(2,1)S(1)}, bf16[864,128]{1,0:T(8,128)(2,1)}, u32[]{:S(2)}) copy-start(bf16[864,128]{1,0:T(8,128)(2,1)} %param.5) | copy-start | bytes 663556
  106.4 8.4 %collective-permute-start.1 = (bf16[1,32,16,128]{3,0,2,1:T(2,128)(2,1)S(1)}, bf16[1,32,16,128]{3,0,2,1:T(2,128)(2,1)S(1)}, u32[]{:S(2)}, u32[]{:S(2)}) collective-permute-start(bf16[1,32,16,128]{3,0,2,1:T(2,128)(2,1)S(1)} %copy.174), channel_id=1, source_target_pairs={{0,1},{1,2},{2,3},{3,4},{4,5},{5,6},{6,7},{8,9},{9,10},{10,11},{11... | collective-permute-start | bytes 393224 | tf_op jit(solution)/shard_map/ppermute | solution.py:10
  125.1 146.5 %reduce-scatter.5.cloned.1.call-start = ((), (), s32[]{:S(2)}) async-start(), calls=%async_computation.4 | async-start | bytes 516096 | tf_op jit(solution)/shard_map/reduce_scatter | solution.py:117
  127.9 191.4 %all-reduce.15.cloned.1.call-start = ((), (), s32[]{:S(2)}) async-start(), calls=%async_computation.5 | async-start | bytes 3538944 | tf_op jit(solution)/shard_map/psum | solution.py:115
Sparse Core Ops, SparseCore 0:
  125.2 81.5 reduce-scatter.6
  210.1 61.4 reduce-scatter.4
  274.1 45.1 all-reduce.14
where the time goes:
time: 330 us; the launch traced here: 329 us
  waiting for transfers between devices  167 us (51%)
  local copies, waits for them, and re-layouts  92.2 us (28%)
  blocking collectives  23.6 us (7%)
  starting transfers between devices  17.5 us (5%)
  between operations  14.3 us (4%)
  other arithmetic  7.38 us (2%)
  matrix products  7.11 us (2%)
    unnamed x4, waiting for transfers between devices  78.9 us
    reduce_scatter x1, waiting for transfers between devices, on_device(): lax.psum_scatter(summed[0], 'space', scatter_dimension=0, tiled=True)  48.2 us
    slice x31, local copies, waits for them, and re-layouts, patches(): lax.slice(phased, start, limit).reshape(out_x, out_y, out_z, channels)  44.7 us
    psum x1, waiting for transfers between devices, on_device(): summed = lax.psum((term_one, term_two), 'dp')  35.4 us
    unnamed x47, local copies, waits for them, and re-layouts  20.1 us
    psum x1, blocking collectives, on_device(): summed = lax.psum((term_one, term_two), 'dp')  12.4 us
    all_to_all x1, blocking collectives, on_device(): lax.all_to_all(latent_slab, 'space', split_axis=0, concat_axis=1, tiled=T...  11.2 us
    ppermute x3, starting transfers between devices, from_behind(): return lax.ppermute(block, axis, route)  10.2 us
  transfers between devices with their start and end apart: 7, of which 5 were waited for; matrix products, arithmetic and copies ran while one was open for 26% of the time, Pallas kernels for 0%

commit v1 on v0

--- a/solution.py
+++ b/solution.py
@@ -94,7 +94,19 @@
     )
     latent_slab = latent_rows.reshape(quarter_x, -1, out_width).transpose(2, 0, 1)
     latent = lax.all_to_all(latent_slab, "space", split_axis=0, concat_axis=1, tiled=True)[None]
-    upstream = lax.all_to_all(cotangent[0], "space", split_axis=1, concat_axis=0, tiled=True)
+    ways, here = (lax.axis_size("space"), lax.axis_index("space"))
+    width = cotangent[0].shape[1] // ways
+    dims = list(cotangent[0].shape)
+    dims[1] = width
+    height = dims[0]
+    dims[0] = height * ways
+    full = jnp.zeros(dims, cotangent[0].dtype)
+    for mask in range(ways):
+        part = lax.dynamic_slice_in_dim(cotangent[0], (here ^ mask) * width, width, axis=1)
+        if mask:
+            part = lax.ppermute(part, "space", [(d, d ^ mask) for d in range(ways)])
+        full = lax.dynamic_update_slice_in_dim(full, part, (here ^ mask) * height, axis=0)
+    upstream = full
     grad_grid = upstream.transpose(1, 2, 0)
     grad_rows = grad_grid.reshape(-1, out_width)
     term_two = lax.dot_general(

time: 330 us -> 319 us (0.967)
  waiting for transfers between devices: 167 us -> 156 us
  local copies, waits for them, and re-layouts: 92.2 us -> 86.2 us
  starting transfers between devices: 17.5 us -> 22.5 us
    reduce_scatter x0 -> x1, waiting for transfers between devices: none -> 79.5 us  [on_device(): lax.psum_scatter(summed[1], 'space', scatter_dimension=0, tiled=True)]
    unnamed x4 -> x3, waiting for transfers between devices: 78.9 us -> 0.05 us
    psum x1, waiting for transfers between devices: 35.4 us -> 21.9 us  [on_device(): summed = lax.psum((term_one, term_two), 'dp')]
    ppermute x0 -> x7, starting transfers between devices: none -> 12.6 us  [on_device(): part = lax.ppermute(part, 'space', [(d, d ^ mask) for d in range(ways)])]
    unnamed x47 -> x52, local copies, waits for them, and re-layouts: 20.1 us -> 9.6 us
    all_to_all x1 -> x0, starting transfers between devices: 7.25 us -> none  [on_device(): lax.all_to_all(cotangent[0], 'space', split_axis=1, concat_axis=0, tiled=...]
  transfers between devices with their start and end apart: 7 -> 13, of which waited for: 5 -> 4; matrix products, arithmetic and copies ran while one was open for 26% -> 27% of each run, Pallas kernels for 0% -> 0%
where the time goes in v1:
time: 319 us; the launch traced here: 317 us
  waiting for transfers between devices  156 us (49%)
  local copies, waits for them, and re-layouts  86.2 us (27%)
  blocking collectives  23.3 us (7%)
  starting transfers between devices  22.5 us (7%)
  between operations  14.6 us (5%)
  other arithmetic  7.37 us (2%)
  matrix products  7.08 us (2%)
    reduce_scatter x1, waiting for transfers between devices, on_device(): lax.psum_scatter(summed[1], 'space', scatter_dimension=0, tiled=True)  79.5 us
    reduce_scatter x1, waiting for transfers between devices, on_device(): lax.psum_scatter(summed[0], 'space', scatter_dimension=0, tiled=True)  51.2 us
    slice x31, local copies, waits for them, and re-layouts, patches(): lax.slice(phased, start, limit).reshape(out_x, out_y, out_z, channels)  44.6 us
    psum x1, waiting for transfers between devices, on_device(): summed = lax.psum((term_one, term_two), 'dp')  21.9 us
    ppermute x7, starting transfers between devices, on_device(): part = lax.ppermute(part, 'space', [(d, d ^ mask) for d in range(ways)])  12.6 us
    psum x1, blocking collectives, on_device(): summed = lax.psum((term_one, term_two), 'dp')  12.4 us
    all_to_all x1, blocking collectives, on_device(): lax.all_to_all(latent_slab, 'space', split_axis=0, concat_axis=1, tiled=T...  11 us
    ppermute x3, starting transfers between devices, from_behind(): return lax.ppermute(block, axis, route)  9.83 us
  transfers between devices with their start and end apart: 13, of which 4 were waited for; matrix products, arithmetic and copies ran while one was open for 27% of the time, Pallas kernels for 0%

profile of v1, /device:TPU:0, one launch (start us, length us, event | category | flops | bytes accessed | tf_op | source)
XLA Modules:
  0.0 317.1 jit_solution(17448295521997678428)
XLA Ops:
  7.3 1.4 constant_dynamic-slice_fusion
  8.7 3.0 collective-permute-start.2
  11.7 1.6 collective-permute-start.3
  13.3 3.0 collective-permute-start.5
  16.3 1.3 collective-permute-start.6
  17.6 1.5 copy.185
  19.1 3.7 %collective-permute-start.7 = (bf16[32,1,128]{2,0,1:T(8,128)(2,1)S(1)}, bf16[32,1,128]{2,0,1:T(8,128)(2,1)S(1)}, u32[]{:S(2)}, u32[]{:S(2)}) collective-permute-start(bf16[32,1,128]{2,0,1:T(8,128)(2,1)S(1)} %bitcast.236), channel_id=1, source_target_pairs={{0,6},{1,7},{2,4},{3,5},{4,2},{5,3},{6,0},{7,1},{8,14},{9,15},{10,... | collective-permute-start | bytes 24584 | tf_op jit(solution)/shard_map/ppermute | solution.py:107
  24.5 3.5 %collective-permute-start = (bf16[1,64,1024]{1,2,0:T(8,128)(2,1)S(1)}, bf16[1,64,1024]{1,2,0:T(8,128)(2,1)S(1)}, u32[]{:S(2)}, u32[]{:S(2)}) collective-permute-start(bf16[1,64,1024]{1,2,0:T(8,128)(2,1)S(1)} %slice_bitcast_fusion.9), channel_id=1, source_target_pairs={{0,1},{1,2},{2,3},{3,4},{4,5},{5,6},{6,7},{8,9},{9,10},{10,11},{11... | collective-permute-start | bytes 393224 | tf_op jit(solution)/shard_map/ppermute | solution.py:10
  36.1 1.1 copy-done.3
  37.1 1.2 fusion.13
  38.3 1.5 collective-permute-start.9
  39.8 1.3 pad_maximum_fusion.2
  41.1 3.9 %copy.286 = bf16[5,64,32,32]{3,1,2,0:T(8,128)(2,1)} copy(bf16[5,64,32,32]{1,3,2,0:T(8,128)(2,1)} %pad_maximum_fusion.2) | data formatting | bytes 1310720
  45.0 4.9 %pad.74 = bf16[6,66,34,32]{3,1,2,0:T(8,128)(2,1)} pad(bf16[5,64,32,32]{3,1,2,0:T(8,128)(2,1)} %copy.286, bf16[]{:T(256)} %constant.15.clone.1), padding=0_1x1_1x1_1x0_0 | pad | bytes 1517058 | tf_op jit(solution)/shard_map/jit(_pad)/pad | solution.py:15
  50.0 8.2 %reshape.221 = bf16[3,2,33,2,17,2,32]{6,3,2,5,4,1,0:T(2,128)(2,1)} reshape(bf16[6,66,34,32]{3,1,2,0:T(8,128)(2,1)} %pad.74) | data formatting | bytes 1723392 | tf_op jit(solution)/shard_map/reshape | solution.py:16
  58.2 15.0 %fusion.11 = (bf16[2,1,32,1,16,1,32]{6,3,2,5,4,1,0:T(2,128)(2,1)S(1)}, bf16[2,1,32,1,16,1,32]{6,3,2,5,4,1,0:T(2,128)(2,1)S(1)}, bf16[2,1,32,1,16,1,32]{6,3,2,5,4...) fusion(bf16[3,2,33,2,17,2,32]{6,3,2,5,4,1,0:T(2,128)(2,1)} %res, ...), kind=kLoop, calls=%fused_computation.83 | loop fusion | bytes 2490368 | tf_op jit(solution)/shard_map/slice | solution.py:32
  73.3 5.1 %fusion.12 = (bf16[2,1,32,1,16,1,32]{6,3,2,5,4,1,0:T(2,128)(2,1)S(1)}, bf16[2,1,32,1,16,1,32]{6,3,2,5,4,1,0:T(2,128)(2,1)S(1)}, bf16[2,1,32,1,16,1,32]{6,3,2,5,4...) fusion(bf16[3,2,33,2,17,2,32]{6,3,2,5,4,1,0:T(2,128)(2,1)S(1)} , ...), kind=kLoop, calls=%fused_computation.84 | loop fusion | bytes 1048576 | tf_op jit(solution)/shard_map/slice | solution.py:32
  89.4 1.0 copy.211
  100.6 1.0 copy.194
  101.7 7.9 %concatenate.153 = bf16[1024,864]{1,0:T(8,128)(2,1)} concatenate(bf16[1024,32]{1,0:T(8,128)(2,1)} %bitcast.223, bf16[1024,32]{1,0:T(8,128)(2,1)} %bitcast.224, bf16[1024,32]{1,0:T(8,128)(2,1)} %bitcast.225, bf16[1024,32]{1,0:T(8,128)(2,1)} %bitcast.226, bf16[1024,32]{1,0:T(8,128)(2,1)} %bitcast.227, bf16[1024,32]{1,0:T(8,128)(2,1)} %bitcast.228, bf16[1024,32]{1,0:T(8,128)(2,1)} %bitcast.229, ...), dimensions={1} | concatenate | bytes 3538944 | tf_op jit(solution)/shard_map/concatenate | solution.py:34
  109.6 1.9 slice_add_fusion
  111.5 1.4 pad_maximum_fusion.4
  114.0 4.8 %collective-permute-start.1 = (bf16[1,32,16,128]{3,0,2,1:T(2,128)(2,1)S(1)}, bf16[1,32,16,128]{3,0,2,1:T(2,128)(2,1)S(1)}, u32[]{:S(2)}, u32[]{:S(2)}) collective-permute-start(bf16[1,32,16,128]{3,0,2,1:T(2,128)(2,1)S(1)} %copy.215), channel_id=1, source_target_pairs={{0,1},{1,2},{2,3},{3,4},{4,5},{5,6},{6,7},{8,9},{9,10},{10,11},{11... | collective-permute-start | bytes 393224 | tf_op jit(solution)/shard_map/ppermute | solution.py:10
  119.1 3.3 %collective-permute-done.1 = bf16[1,32,16,128]{3,0,2,1:T(2,128)(2,1)S(1)} collective-permute-done((bf16[1,32,16,128]{3,0,2,1:T(2,128)(2,1)S(1)}, bf16[1,32,16,128]{3,0,2,1:T(2,128)(2,1)S(1)}, u32[]{:S(2)}, u32[]{:S(2)}) %collective-permute-start.1) | collective-permute-done | bytes 131104 | tf_op jit(solution)/shard_map/ppermute | solution.py:10
  125.0 2.4 fusion.8
  127.5 2.7 fusion.16
  130.4 79.5 %reduce-scatter.5.cloned.1.call-done = f32[32,3456]{1,0:T(8,128)} async-done(((f32[256,3456]{1,0:T(8,128)}), f32[32,3456]{1,0:T(8,128)}) %reduce-scatter.5.cloned.1.call-update) | async-done | bytes 442384 | tf_op jit(solution)/shard_map/reduce_scatter | solution.py:130
  211.6 11.0 %all_to_all.15 = bf16[8,2,2048]{2,1,0:T(2,128)(2,1)S(1)} all-to-all(bf16[8,2,2048]{2,1,0:T(2,128)(2,1)S(1)} %reshape.233), channel_id=1, replica_groups=mesh['dp'=4,'space'=8] {'space'}, dimensions={0} | all-to-all | bytes 131072 | tf_op jit(solution)/shard_map/all_to_all | solution.py:96
  223.3 51.2 %reduce-scatter.3.cloned.1.call-done = f32[16,864]{1,0:T(8,128)} async-done(((f32[128,864]{1,0:T(8,128)}), f32[16,864]{1,0:T(8,128)}) %reduce-scatter.3.cloned.1.call-update) | async-done | bytes 55312 | tf_op jit(solution)/shard_map/reduce_scatter | solution.py:129
  274.6 12.4 %psum.16 = f32[16,864]{1,0:T(8,128)} all-reduce(f32[16,864]{1,0:T(8,128)} %reduce-scatter.3.cloned.1.call-done), channel_id=1, replica_groups=mesh['dp'=4,'space'=8] {'dp'}, use_global_device_ids=true, to_apply=%region_0.1 | all-reduce | flops 13824 | bytes 110592 | tf_op jit(solution)/shard_map/psum | solution.py:127
  286.9 21.9 %all-reduce.15.cloned.1.call-done = f32[32,3456]{1,0:T(8,128)} async-done(((f32[32,3456]{1,0:T(8,128)}), f32[32,3456]{1,0:T(8,128)}) %all-reduce.15.cloned.1.call-update) | async-done | bytes 442384 | tf_op jit(solution)/shard_map/psum | solution.py:127
  308.8 1.8 copy.366
  (136 shorter events, 37.0 us)
Async XLA Ops:
  7.2 23.4 %copy-start = (bf16[3456,256]{1,0:T(8,128)(2,1)S(1)}, bf16[3456,256]{1,0:T(8,128)(2,1)}, u32[]{:S(2)}) copy-start(bf16[3456,256]{1,0:T(8,128)(2,1)} %param.6) | copy-start | bytes 5308420
  7.2 202.7 %reduce-scatter.5.cloned.1.call-start = ((), (), s32[]{:S(2)}) async-start(), calls=%async_computation.4 | async-start | bytes 3981312 | tf_op jit(solution)/shard_map/reduce_scatter | solution.py:130
  8.7 10.4 %collective-permute-start.2 = (bf16[32,1,128]{2,0,1:T(8,128)(2,1)S(1)}, bf16[32,1,128]{2,0,1:T(8,128)(2,1)S(1)}, u32[]{:S(2)}, u32[]{:S(2)}) collective-permute-start(bf16[32,1,128]{2,0,1:T(8,128)(2,1)S(1)} %bitcast.241), channel_id=1, source_target_pairs={{0,1},{1,0},{2,3},{3,2},{4,5},{5,4},{6,7},{7,6},{8,9},{9,8},{10,11... | collective-permute-start | bytes 24584 | tf_op jit(solution)/shard_map/ppermute | solution.py:107
  11.7 11.1 %collective-permute-start.3 = (bf16[32,1,128]{2,0,1:T(8,128)(2,1)S(1)}, bf16[32,1,128]{2,0,1:T(8,128)(2,1)S(1)}, u32[]{:S(2)}, u32[]{:S(2)}) collective-permute-start(bf16[32,1,128]{2,0,1:T(8,128)(2,1)S(1)} %bitcast.240), channel_id=1, source_target_pairs={{0,2},{1,3},{2,0},{3,1},{4,6},{5,7},{6,4},{7,5},{8,10},{9,11},{10,... | collective-permute-start | bytes 24584 | tf_op jit(solution)/shard_map/ppermute | solution.py:107
  13.3 11.2 %collective-permute-start.4 = (bf16[32,1,128]{2,0,1:T(8,128)(2,1)S(1)}, bf16[32,1,128]{2,0,1:T(8,128)(2,1)S(1)}, u32[]{:S(2)}, u32[]{:S(2)}) collective-permute-start(bf16[32,1,128]{2,0,1:T(8,128)(2,1)S(1)} %bitcast.239), channel_id=1, source_target_pairs={{0,3},{1,2},{2,1},{3,0},{4,7},{5,6},{6,5},{7,4},{8,11},{9,10},{10,... | collective-permute-start | bytes 24584 | tf_op jit(solution)/shard_map/ppermute | solution.py:107
  13.3 15.3 %collective-permute-start.5 = (bf16[32,1,128]{2,0,1:T(8,128)(2,1)S(1)}, bf16[32,1,128]{2,0,1:T(8,128)(2,1)S(1)}, u32[]{:S(2)}, u32[]{:S(2)}) collective-permute-start(bf16[32,1,128]{2,0,1:T(8,128)(2,1)S(1)} %bitcast.238), channel_id=1, source_target_pairs={{0,4},{1,5},{2,6},{3,7},{4,0},{5,1},{6,2},{7,3},{8,12},{9,13},{10,... | collective-permute-start | bytes 24584 | tf_op jit(solution)/shard_map/ppermute | solution.py:107
  16.3 12.6 %collective-permute-start.6 = (bf16[32,1,128]{2,0,1:T(8,128)(2,1)S(1)}, bf16[32,1,128]{2,0,1:T(8,128)(2,1)S(1)}, u32[]{:S(2)}, u32[]{:S(2)}) collective-permute-start(bf16[32,1,128]{2,0,1:T(8,128)(2,1)S(1)} %bitcast.237), channel_id=1, source_target_pairs={{0,5},{1,4},{2,7},{3,6},{4,1},{5,0},{6,3},{7,2},{8,13},{9,12},{10,... | collective-permute-start | bytes 24584 | tf_op jit(solution)/shard_map/ppermute | solution.py:107
  19.1 10.3 %collective-permute-start.7 = (bf16[32,1,128]{2,0,1:T(8,128)(2,1)S(1)}, bf16[32,1,128]{2,0,1:T(8,128)(2,1)S(1)}, u32[]{:S(2)}, u32[]{:S(2)}) collective-permute-start(bf16[32,1,128]{2,0,1:T(8,128)(2,1)S(1)} %bitcast.236), channel_id=1, source_target_pairs={{0,6},{1,7},{2,4},{3,5},{4,2},{5,3},{6,0},{7,1},{8,14},{9,15},{10,... | collective-permute-start | bytes 24584 | tf_op jit(solution)/shard_map/ppermute | solution.py:107
  22.8 7.2 %collective-permute-start.8 = (bf16[32,1,128]{2,0,1:T(8,128)(2,1)S(1)}, bf16[32,1,128]{2,0,1:T(8,128)(2,1)S(1)}, u32[]{:S(2)}, u32[]{:S(2)}) collective-permute-start(bf16[32,1,128]{2,0,1:T(8,128)(2,1)S(1)} %bitcast.235), channel_id=1, source_target_pairs={{0,7},{1,6},{2,5},{3,4},{4,3},{5,2},{6,1},{7,0},{8,15},{9,14},{10,... | collective-permute-start | bytes 24584 | tf_op jit(solution)/shard_map/ppermute | solution.py:107
  24.5 15.3 %collective-permute-start = (bf16[1,64,1024]{1,2,0:T(8,128)(2,1)S(1)}, bf16[1,64,1024]{1,2,0:T(8,128)(2,1)S(1)}, u32[]{:S(2)}, u32[]{:S(2)}) collective-permute-start(bf16[1,64,1024]{1,2,0:T(8,128)(2,1)S(1)} %slice_bitcast_fusion.9), channel_id=1, source_target_pairs={{0,1},{1,2},{2,3},{3,4},{4,5},{5,6},{6,7},{8,9},{9,10},{10,11},{11... | collective-permute-start | bytes 393224 | tf_op jit(solution)/shard_map/ppermute | solution.py:10
  36.1 1.1 copy-start.3
  38.3 71.3 %collective-permute-start.9 = (f32[1,32,16,128]{3,0,2,1:T(1,128)}, f32[1,32,16,128]{3,0,2,1:T(1,128)}, u32[]{:S(2)}, u32[]{:S(2)}) collective-permute-start(f32[1,32,16,128]{3,0,2,1:T(1,128)} %get-tuple-element.49), channel_id=1, source_target_pairs={{1,0},{2,1},{3,2},{4,3},{5,4},{6,5},{7,6},{9,8},{10,9},{11,10},{12... | collective-permute-start | bytes 786440 | tf_op jit(solution)/shard_map/ppermute | solution.py:10
  58.2 15.0 %copy-start.1 = (bf16[3,2,33,2,17,2,32]{6,3,2,5,4,1,0:T(2,128)(2,1)S(1)}, bf16[3,2,33,2,17,2,32]{6,3,2,5,4,1,0:T(2,128)(2,1)}, u32[]{:S(2)}) copy-start(bf16[3,2,33,2,17,2,32]{6,3,2,5,4,1,0:T(2,128)(2,1)} %reshape.221) | copy-start | bytes 2585092
  109.6 3.4 %copy-start.2 = (bf16[1024,864]{1,0:T(8,128)(2,1)S(1)}, bf16[1024,864]{1,0:T(8,128)(2,1)}, u32[]{:S(2)}) copy-start(bf16[1024,864]{1,0:T(8,128)(2,1)} %concatenate.153) | copy-start | bytes 5308420
  109.6 3.4 %copy-start.4 = (bf16[864,128]{1,0:T(8,128)(2,1)S(1)}, bf16[864,128]{1,0:T(8,128)(2,1)}, u32[]{:S(2)}) copy-start(bf16[864,128]{1,0:T(8,128)(2,1)} %param.5) | copy-start | bytes 663556
  114.0 8.4 %collective-permute-start.1 = (bf16[1,32,16,128]{3,0,2,1:T(2,128)(2,1)S(1)}, bf16[1,32,16,128]{3,0,2,1:T(2,128)(2,1)S(1)}, u32[]{:S(2)}, u32[]{:S(2)}) collective-permute-start(bf16[1,32,16,128]{3,0,2,1:T(2,128)(2,1)S(1)} %copy.215), channel_id=1, source_target_pairs={{0,1},{1,2},{2,3},{3,4},{4,5},{5,6},{6,7},{8,9},{9,10},{10,11},{11... | collective-permute-start | bytes 393224 | tf_op jit(solution)/shard_map/ppermute | solution.py:10
  127.5 147.1 %reduce-scatter.3.cloned.1.call-start = ((), (), s32[]{:S(2)}) async-start(), calls=%async_computation.3 | async-start | bytes 516096 | tf_op jit(solution)/shard_map/reduce_scatter | solution.py:129
  130.3 178.5 %all-reduce.15.cloned.1.call-start = ((), (), s32[]{:S(2)}) async-start(), calls=%async_computation.5 | async-start | bytes 884736 | tf_op jit(solution)/shard_map/psum | solution.py:127
Sparse Core Ops, SparseCore 0:
  127.6 82.2 reduce-scatter.4
  213.1 61.3 reduce-scatter.2
  277.1 31.6 all-reduce.14
